TPU v7x, 256 devices: a whole 4x4x8 slice. The times are simulated.
256 devices in a mesh: section: 64 (over z_lo, x, y, core), tensor: 4 (over z_hi).
Axes of the slice: x: 4, y: 4, z: 8 (z_hi: 4, z_lo: 2; z = z_hi * 2 + z_lo), core: 2. Of those that a mesh axis runs over, the one named last changes fastest.
Arguments:
- key_weight: bfloat16 [64, 4096, 512], P('section', None, 'tensor'), may hold values from -0.046875 to 0.046875
- first_moment: float32 [64, 4096, 512], P('section', None, 'tensor'), may hold values from -3 to 3
- second_moment: float32 [64, 4096, 512], P('section', None, 'tensor'), may hold values from 0.05 to 2
- down_inputs: bfloat16 [64, 256, 4096], P('section', None, 'tensor'), may hold values from -0.59765625 to 0.59765625
- up_inputs: bfloat16 [64, 256, 4096], P('section', None, 'tensor'), may hold values from -0.59765625 to 0.59765625
- down_key_grads: bfloat16 [64, 256, 512], P('section', None, 'tensor'), may hold values from -6 to 6
- up_key_grads: bfloat16 [64, 256, 512], P('section', None, 'tensor'), may hold values from -6 to 6
Outputs:
- new_weight: float32 [64, 4096, 512], P('section', None, 'tensor')
- new_first: float32 [64, 4096, 512], P('section', None, 'tensor')
- new_second: float32 [64, 4096, 512], P('section', None, 'tensor')
- down_received: bfloat16 [64, 4096, 256], P('section', 'tensor')
- up_received: bfloat16 [64, 4096, 256], P('section', 'tensor')
All inputs are finite; a program needn't handle non-finite values.
Results may differ from a plain program's by a relative error of at most 0.006.
Values may be sent and summed in bfloat16 or wider, within the bound.
A program may use at most 128 MiB of HBM per device.

v0:
```python
import jax
import jax.numpy as jnp
from jax import lax
from jax.sharding import PartitionSpec as P

ADAM_STEP = 100


beta_one = 0.9
beta_two = 0.95
learn_rate = 0.00015
decay_rate = 0.1
epsilon = 1e-08


def from_partner(block, axis, stride):
    count = lax.axis_size(axis)
    route = []
    for low in range(count):
        high = low | 1 << stride
        if high != low and high < count:
            route += [(low, high), (high, low)]
    return lax.ppermute(block, axis, route)


def passed_along(value, axis, by):
    length = lax.axis_size(axis)
    pairs = [(i, i + by) for i in range(length) if 0 <= i + by < length]
    return lax.ppermute(value, axis, pairs)


def column_grad(key_grads, shard_piece):
    return lax.dot_general(
        shard_piece, key_grads, (((0,), (0,)), ((), ())), preferred_element_type=jnp.float32
    )


def input_term(rows_weight, key_grads):
    summed = lax.psum_scatter(
        lax.dot_general(
            rows_weight, key_grads, (((1,), (1,)), ((), ())), preferred_element_type=jnp.float32
        ),
        "tensor",
        scatter_dimension=0,
        tiled=True,
    )
    return summed.astype(jnp.bfloat16)


def local(
    key_weight, first_moment, second_moment, down_inputs, up_inputs, down_key_grads, up_key_grads
):
    weight = key_weight[0]
    down_rows = down_inputs[0]
    up_rows = up_inputs[0]
    down_grads = down_key_grads[0]
    up_grads = up_key_grads[0]
    bit_count = lax.axis_size("section").bit_length() - 1
    swap_order = list(range(bit_count))
    mirror_weight = weight
    for bit_index in swap_order:
        mirror_weight = from_partner(mirror_weight, "section", bit_index)
    down_grad = column_grad(down_grads, lax.all_gather(down_rows, "tensor", axis=1, tiled=True))
    up_grad = column_grad(up_grads, lax.all_gather(up_rows, "tensor", axis=1, tiled=True))
    for bit_index in swap_order:
        up_grad = from_partner(up_grad.astype(jnp.bfloat16), "section", bit_index).astype(
            up_grad.dtype
        )
    gradient = down_grad + up_grad
    new_first = beta_one * first_moment[0] + (1.0 - beta_one) * gradient
    new_second = beta_two * second_moment[0] + (1.0 - beta_two) * gradient * gradient
    first_hat = new_first / (1.0 - beta_one**ADAM_STEP)
    second_hat = new_second / (1.0 - beta_two**ADAM_STEP)
    weight_full = weight.astype(jnp.float32)
    new_weight = weight_full - learn_rate * (
        first_hat / (jnp.sqrt(second_hat) + epsilon) + decay_rate * weight_full
    )
    down_term = input_term(weight, down_grads)
    up_term = input_term(mirror_weight, up_grads)
    down_received = passed_along(down_term, "section", -1)
    up_received = passed_along(up_term, "section", 1)
    return (
        new_weight[None],
        new_first[None],
        new_second[None],
        down_received[None],
        up_received[None],
    )


def solution(mesh):
    in_specs = (
        P("section", None, "tensor"),
        P("section", None, "tensor"),
        P("section", None, "tensor"),
        P("section", None, "tensor"),
        P("section", None, "tensor"),
        P("section", None, "tensor"),
        P("section", None, "tensor"),
    )
    out_specs = (
        P("section", None, "tensor"),
        P("section", None, "tensor"),
        P("section", None, "tensor"),
        P("section", "tensor", None),
        P("section", "tensor", None),
    )
    return jax.shard_map(local, mesh=mesh, in_specs=in_specs, out_specs=out_specs, check_vma=False)
```

profile of v0, /device:TPU:32, one launch (start us, length us, event | category | flops | bytes accessed | tf_op | source)
XLA Modules:
  0.0 347.6 jit_solution(14269661047280779210)
XLA Ops:
  8.0 3.9 %fusion.10 = f32[4096,256]{1,0:T(8,128)} fusion(bf16[1,256,128]{2,1,0:T(8,128)(2,1)} %param.12, bf16[1,4096,128]{2,1,0:T(8,128)(2,1)} %param.7), kind=kOutput, calls=%fused_computation.16 | convolution fusion | flops 268435456 | bytes 5308416 | tf_op jit(solution)/shard_map/dot_general | solution.py:40
  13.1 2.7 collective-permute-done.7
  15.8 1.6 collective-permute-start.8
  17.4 23.6 %collective-permute-done.8 = bf16[4096,128]{1,0:T(8,128)(2,1)S(1)} collective-permute-done((bf16[4096,128]{1,0:T(8,128)(2,1)S(1)}, bf16[4096,128]{1,0:T(8,128)(2,1)S(1)}, u32[]{:S(2)}, u32[]{:S(2)}) %collective-permute-start.8) | collective-permute-done | bytes 1048608 | tf_op jit(solution)/shard_map/ppermute | solution.py:23
  41.0 3.2 collective-permute-start.9
  44.2 22.8 %collective-permute-done.9 = bf16[4096,128]{1,0:T(8,128)(2,1)S(1)} collective-permute-done((bf16[4096,128]{1,0:T(8,128)(2,1)S(1)}, bf16[4096,128]{1,0:T(8,128)(2,1)S(1)}, u32[]{:S(2)}, u32[]{:S(2)}) %collective-permute-start.9) | collective-permute-done | bytes 1048608 | tf_op jit(solution)/shard_map/ppermute | solution.py:23
  67.0 1.5 collective-permute-start.10
  68.5 22.0 %collective-permute-done.10 = bf16[4096,128]{1,0:T(8,128)(2,1)S(1)} collective-permute-done((bf16[4096,128]{1,0:T(8,128)(2,1)S(1)}, bf16[4096,128]{1,0:T(8,128)(2,1)S(1)}, u32[]{:S(2)}, u32[]{:S(2)}) %collective-permute-start.10) | collective-permute-done | bytes 1048608 | tf_op jit(solution)/shard_map/ppermute | solution.py:23
  90.5 3.0 collective-permute-start.11
  93.5 21.6 %collective-permute-done.11 = bf16[4096,128]{1,0:T(8,128)(2,1)S(1)} collective-permute-done((bf16[4096,128]{1,0:T(8,128)(2,1)S(1)}, bf16[4096,128]{1,0:T(8,128)(2,1)S(1)}, u32[]{:S(2)}, u32[]{:S(2)}) %collective-permute-start.11) | collective-permute-done | bytes 1048608 | tf_op jit(solution)/shard_map/ppermute | solution.py:23
  115.2 1.4 collective-permute-start.12
  116.6 51.6 %collective-permute-done.12 = bf16[4096,128]{1,0:T(8,128)(2,1)S(1)} collective-permute-done((bf16[4096,128]{1,0:T(8,128)(2,1)S(1)}, bf16[4096,128]{1,0:T(8,128)(2,1)S(1)}, u32[]{:S(2)}, u32[]{:S(2)}) %collective-permute-start.12) | collective-permute-done | bytes 1048608 | tf_op jit(solution)/shard_map/ppermute | solution.py:23
  168.2 2.7 fusion.7
  170.9 2.4 convolution_convert_fusion
  173.4 2.6 collective-permute-done
  176.0 2.4 collective-permute-start.1
  178.5 23.5 %collective-permute-done.1 = bf16[4096,128]{1,0:T(8,128)(2,1)S(1)} collective-permute-done((bf16[4096,128]{1,0:T(8,128)(2,1)S(1)}, bf16[4096,128]{1,0:T(8,128)(2,1)S(1)}, u32[]{:S(2)}, u32[]{:S(2)}) %collective-permute-start.1) | collective-permute-done | bytes 1048608 | tf_op jit(solution)/shard_map/ppermute | solution.py:23
  201.9 2.7 collective-permute-start.2
  204.6 23.6 %collective-permute-done.2 = bf16[4096,128]{1,0:T(8,128)(2,1)S(1)} collective-permute-done((bf16[4096,128]{1,0:T(8,128)(2,1)S(1)}, bf16[4096,128]{1,0:T(8,128)(2,1)S(1)}, u32[]{:S(2)}, u32[]{:S(2)}) %collective-permute-start.2) | collective-permute-done | bytes 1048608 | tf_op jit(solution)/shard_map/ppermute | solution.py:23
  228.2 1.4 collective-permute-start.3
  229.7 22.5 %collective-permute-done.3 = bf16[4096,128]{1,0:T(8,128)(2,1)S(1)} collective-permute-done((bf16[4096,128]{1,0:T(8,128)(2,1)S(1)}, bf16[4096,128]{1,0:T(8,128)(2,1)S(1)}, u32[]{:S(2)}, u32[]{:S(2)}) %collective-permute-start.3) | collective-permute-done | bytes 1048608 | tf_op jit(solution)/shard_map/ppermute | solution.py:23
  252.1 2.6 collective-permute-start.4
  254.7 22.1 %collective-permute-done.4 = bf16[4096,128]{1,0:T(8,128)(2,1)} collective-permute-done((bf16[4096,128]{1,0:T(8,128)(2,1)S(1)}, bf16[4096,128]{1,0:T(8,128)(2,1)}, u32[]{:S(2)}, u32[]{:S(2)}) %collective-permute-start.4) | collective-permute-done | bytes 1048608 | tf_op jit(solution)/shard_map/ppermute | solution.py:23
  276.8 2.1 convert_element_type.13
  278.9 3.9 %collective-permute-start.6 = (bf16[1024,256]{1,0:T(8,128)(2,1)}, bf16[1024,256]{1,0:T(8,128)(2,1)}, u32[]{:S(2)}, u32[]{:S(2)}) collective-permute-start(bf16[1024,256]{1,0:T(8,128)(2,1)} %convert_element_type.13), channel_id=1, source_target_pairs={{4,0},{8,4},{12,8},{16,12},{20,16},{24,20},{28,24},{32,28},{36,32}... | collective-permute-start | bytes 1572872 | tf_op jit(solution)/shard_map/ppermute | solution.py:29
  282.9 2.4 fusion.5
  285.3 37.0 %collective-permute-done.6 = bf16[1024,256]{1,0:T(8,128)(2,1)} collective-permute-done((bf16[1024,256]{1,0:T(8,128)(2,1)}, bf16[1024,256]{1,0:T(8,128)(2,1)}, u32[]{:S(2)}, u32[]{:S(2)}) %collective-permute-start.6) | collective-permute-done | bytes 524320 | tf_op jit(solution)/shard_map/ppermute | solution.py:29
  322.2 1.3 convert_element_type.14
  323.5 1.9 collective-permute-start.13
  325.5 7.0 %fusion.15 = (f32[1,4096,128]{2,1,0:T(8,128)}, f32[1,4096,128]{2,1,0:T(8,128)}, f32[1,4096,128]{2,1,0:T(8,128)}) fusion(f32[4096,128]{1,0:T(8,128)S(1)} %fusion.5, bf16[4096,128]{1,0:T(8,128)(2,1)} %collective-permute-done.5, f32[1,4096,128]{2,1,0:T(8,128)} %param.9, f32[1,4096,128]{2,1,0:T(8,128)} %param.8, bf16[1,4096,128]{2,1,0:T(8,128)(2,1)S(1)} %copy-done.1), kind=kLoop, calls=%fused_computation.21 | loop fusion | flops 9437184 | bytes 14680064 | tf_op jit(solution)/shard_map/broadcast_in_dim | solution.py:85
  332.4 6.0 %collective-permute-done.13 = bf16[1024,256]{1,0:T(8,128)(2,1)S(1)} collective-permute-done((bf16[1024,256]{1,0:T(8,128)(2,1)S(1)}, bf16[1024,256]{1,0:T(8,128)(2,1)S(1)}, u32[]{:S(2)}, u32[]{:S(2)}) %collective-permute-start.13) | collective-permute-done | bytes 524320 | tf_op jit(solution)/shard_map/ppermute | solution.py:29
  338.4 1.9 copy.14
  (23 shorter events, 3.0 us)
Async XLA Ops:
  7.2 161.0 %copy-start = (bf16[1,256,128]{2,1,0:T(8,128)(2,1)S(1)}, bf16[1,256,128]{2,1,0:T(8,128)(2,1)}, u32[]{:S(2)}) copy-start(bf16[1,256,128]{2,1,0:T(8,128)(2,1)} %param.13) | copy-start | bytes 196612
  7.2 163.7 %all-gather.7.cloned.1.call-start = ((), (), s32[]{:S(2)}) async-start(), calls=%async_computation.5 | async-start | bytes 2621440 | tf_op jit(solution)/shard_map/all_gather | solution.py:64
  7.9 268.9 %reduce-scatter.3.cloned.1.call-start = ((), (), s32[]{:S(2)}) async-start(), calls=%async_computation.2 | async-start | bytes 5242880 | tf_op jit(solution)/shard_map/reduce_scatter | solution.py:39
  11.9 1.2 copy-start.1
  11.9 271.0 %all-gather.5.cloned.1.call-start = ((), (), s32[]{:S(2)}) async-start(), calls=%async_computation.4 | async-start | bytes 2621440 | tf_op jit(solution)/shard_map/all_gather | solution.py:63
  13.1 2.7 collective-permute-start.7
  15.8 25.2 %collective-permute-start.8 = (bf16[4096,128]{1,0:T(8,128)(2,1)S(1)}, bf16[4096,128]{1,0:T(8,128)(2,1)S(1)}, u32[]{:S(2)}, u32[]{:S(2)}) collective-permute-start(bf16[4096,128]{1,0:T(8,128)(2,1)S(1)} %collective-permute-done.7), channel_id=1, source_target_pairs={{0,8},{8,0},{4,12},{12,4},{16,24},{24,16},{20,28},{28,20},{32,40},... | collective-permute-start | bytes 3145736 | tf_op jit(solution)/shard_map/ppermute | solution.py:23
  41.0 26.0 %collective-permute-start.9 = (bf16[4096,128]{1,0:T(8,128)(2,1)S(1)}, bf16[4096,128]{1,0:T(8,128)(2,1)S(1)}, u32[]{:S(2)}, u32[]{:S(2)}) collective-permute-start(bf16[4096,128]{1,0:T(8,128)(2,1)S(1)} %collective-permute-done.8), channel_id=1, source_target_pairs={{0,16},{16,0},{4,20},{20,4},{8,24},{24,8},{12,28},{28,12},{32,48},... | collective-permute-start | bytes 3145736 | tf_op jit(solution)/shard_map/ppermute | solution.py:23
  67.0 23.6 %collective-permute-start.10 = (bf16[4096,128]{1,0:T(8,128)(2,1)S(1)}, bf16[4096,128]{1,0:T(8,128)(2,1)S(1)}, u32[]{:S(2)}, u32[]{:S(2)}) collective-permute-start(bf16[4096,128]{1,0:T(8,128)(2,1)S(1)} %collective-permute-done.9), channel_id=1, source_target_pairs={{0,32},{32,0},{4,36},{36,4},{8,40},{40,8},{12,44},{44,12},{16,48},... | collective-permute-start | bytes 3145736 | tf_op jit(solution)/shard_map/ppermute | solution.py:23
  68.5 253.8 %reduce-scatter.5.cloned.1.call-start = ((), (), s32[]{:S(2)}) async-start(), calls=%async_computation.3 | async-start | bytes 5242880 | tf_op jit(solution)/shard_map/reduce_scatter | solution.py:39
  90.5 24.7 %collective-permute-start.11 = (bf16[4096,128]{1,0:T(8,128)(2,1)S(1)}, bf16[4096,128]{1,0:T(8,128)(2,1)S(1)}, u32[]{:S(2)}, u32[]{:S(2)}) collective-permute-start(bf16[4096,128]{1,0:T(8,128)(2,1)S(1)} %collective-permute-done.10), channel_id=1, source_target_pairs={{0,64},{64,0},{4,68},{68,4},{8,72},{72,8},{12,76},{76,12},{16,80},... | collective-permute-start | bytes 3145736 | tf_op jit(solution)/shard_map/ppermute | solution.py:23
  115.2 53.0 %collective-permute-start.12 = (bf16[4096,128]{1,0:T(8,128)(2,1)S(1)}, bf16[4096,128]{1,0:T(8,128)(2,1)S(1)}, u32[]{:S(2)}, u32[]{:S(2)}) collective-permute-start(bf16[4096,128]{1,0:T(8,128)(2,1)S(1)} %collective-permute-done.11), channel_id=1, source_target_pairs={{0,128},{128,0},{4,132},{132,4},{8,136},{136,8},{12,140},{140,12},... | collective-permute-start | bytes 3145736 | tf_op jit(solution)/shard_map/ppermute | solution.py:23
  170.9 112.0 %copy-start.2 = (bf16[1,256,128]{2,1,0:T(8,128)(2,1)S(1)}, bf16[1,256,128]{2,1,0:T(8,128)(2,1)}, u32[]{:S(2)}) copy-start(bf16[1,256,128]{2,1,0:T(8,128)(2,1)} %param.12) | copy-start | bytes 196612
  173.3 2.7 collective-permute-start
  176.0 25.9 %collective-permute-start.1 = (bf16[4096,128]{1,0:T(8,128)(2,1)S(1)}, bf16[4096,128]{1,0:T(8,128)(2,1)S(1)}, u32[]{:S(2)}, u32[]{:S(2)}) collective-permute-start(bf16[4096,128]{1,0:T(8,128)(2,1)S(1)} %collective-permute-done), channel_id=1, source_target_pairs={{0,8},{8,0},{4,12},{12,4},{16,24},{24,16},{20,28},{28,20},{32,40},... | collective-permute-start | bytes 3145736 | tf_op jit(solution)/shard_map/ppermute | solution.py:23
  201.9 26.3 %collective-permute-start.2 = (bf16[4096,128]{1,0:T(8,128)(2,1)S(1)}, bf16[4096,128]{1,0:T(8,128)(2,1)S(1)}, u32[]{:S(2)}, u32[]{:S(2)}) collective-permute-start(bf16[4096,128]{1,0:T(8,128)(2,1)S(1)} %collective-permute-done.1), channel_id=1, source_target_pairs={{0,16},{16,0},{4,20},{20,4},{8,24},{24,8},{12,28},{28,12},{32,48},... | collective-permute-start | bytes 3145736 | tf_op jit(solution)/shard_map/ppermute | solution.py:23
  228.2 23.9 %collective-permute-start.3 = (bf16[4096,128]{1,0:T(8,128)(2,1)S(1)}, bf16[4096,128]{1,0:T(8,128)(2,1)S(1)}, u32[]{:S(2)}, u32[]{:S(2)}) collective-permute-start(bf16[4096,128]{1,0:T(8,128)(2,1)S(1)} %collective-permute-done.2), channel_id=1, source_target_pairs={{0,32},{32,0},{4,36},{36,4},{8,40},{40,8},{12,44},{44,12},{16,48},... | collective-permute-start | bytes 3145736 | tf_op jit(solution)/shard_map/ppermute | solution.py:23
  252.1 24.7 %collective-permute-start.4 = (bf16[4096,128]{1,0:T(8,128)(2,1)S(1)}, bf16[4096,128]{1,0:T(8,128)(2,1)}, u32[]{:S(2)}, u32[]{:S(2)}) collective-permute-start(bf16[4096,128]{1,0:T(8,128)(2,1)S(1)} %collective-permute-done.3), channel_id=1, source_target_pairs={{0,64},{64,0},{4,68},{68,4},{8,72},{72,8},{12,76},{76,12},{16,80},... | collective-permute-start | bytes 3145736 | tf_op jit(solution)/shard_map/ppermute | solution.py:23
  276.8 48.6 %collective-permute-start.5 = (bf16[4096,128]{1,0:T(8,128)(2,1)}, bf16[4096,128]{1,0:T(8,128)(2,1)}, u32[]{:S(2)}, u32[]{:S(2)}) collective-permute-start(bf16[4096,128]{1,0:T(8,128)(2,1)} %collective-permute-done.4), channel_id=1, source_target_pairs={{0,128},{128,0},{4,132},{132,4},{8,136},{136,8},{12,140},{140,12},... | collective-permute-start | bytes 3145736 | tf_op jit(solution)/shard_map/ppermute | solution.py:23
  278.9 43.3 %collective-permute-start.6 = (bf16[1024,256]{1,0:T(8,128)(2,1)}, bf16[1024,256]{1,0:T(8,128)(2,1)}, u32[]{:S(2)}, u32[]{:S(2)}) collective-permute-start(bf16[1024,256]{1,0:T(8,128)(2,1)} %convert_element_type.13), channel_id=1, source_target_pairs={{4,0},{8,4},{12,8},{16,12},{20,16},{24,20},{28,24},{32,28},{36,32}... | collective-permute-start | bytes 1572872 | tf_op jit(solution)/shard_map/ppermute | solution.py:29
  323.5 14.9 %collective-permute-start.13 = (bf16[1024,256]{1,0:T(8,128)(2,1)S(1)}, bf16[1024,256]{1,0:T(8,128)(2,1)S(1)}, u32[]{:S(2)}, u32[]{:S(2)}) collective-permute-start(bf16[1024,256]{1,0:T(8,128)(2,1)S(1)} %convert_element_type.14), channel_id=1, source_target_pairs={{0,4},{4,8},{8,12},{12,16},{16,20},{20,24},{24,28},{28,32},{32,36}... | collective-permute-start | bytes 1572872 | tf_op jit(solution)/shard_map/ppermute | solution.py:29
Sparse Core Ops, SparseCore 0:
  9.8 53.3 all-gather.6
  65.8 93.9 reduce-scatter.2
  161.7 51.5 all-gather.4
  215.9 87.3 reduce-scatter.4
where the time goes:
time: 348 us
  waiting for transfers between devices  282 us (81%)
  starting transfers between devices  26 us (7%)
  between operations  13.9 us (4%)
  matrix products  11.3 us (3%)
  other arithmetic  10.3 us (3%)
  local copies, waits for them, and re-layouts  3.83 us (1%)
    ppermute x12, waiting for transfers between devices, from_partner(): return lax.ppermute(block, axis, route)  239 us
    ppermute x2, waiting for transfers between devices, passed_along(): return lax.ppermute(value, axis, pairs)  42.9 us
    ppermute x12, starting transfers between devices, from_partner(): return lax.ppermute(block, axis, route)  20 us
    broadcast_in_dim x1, other arithmetic, local(): new_second[None]  6.99 us
  transfers between devices with their start and end apart: 18, of which 13 were waited for; matrix products, arithmetic and copies ran while one was open for 6% of the time, Pallas kernels for 0%

commit v1 on v0

v1 whole, which is shorter than its diff:
```python
import jax
import jax.numpy as jnp
from jax import lax
from jax.experimental import pallas as pl
from jax.experimental.pallas import tpu as pltpu
from jax.sharding import PartitionSpec as P

ADAM_STEP = 100


beta_one = 0.9
beta_two = 0.95
learn_rate = 0.00015
decay_rate = 0.1
epsilon = 1e-08

MESH = pl.DeviceIdType.MESH
CHUNKS = 4


def relay_kernel(
    sections,
    ways,
    weight,
    down_rows,
    up_rows,
    down_grads,
    up_grads,
    grad_out,
    down_out,
    up_out,
    tokens,
    keys,
    rows,
    grads,
    down_term,
    up_term,
    local_sem,
    key_send,
    key_recv,
    mirror_key_send,
    mirror_key_recv,
    row_send,
    row_recv,
    weight_send,
    weight_recv,
    grad_send,
    grad_recv,
    term_send,
    term_recv,
):
    s = lax.axis_index("section")
    t = lax.axis_index("tensor")
    mirror = sections - 1 - s
    after = sections - s
    toks = down_rows.shape[0]
    feats = down_rows.shape[1]
    cols = down_grads.shape[1]
    step = feats // CHUNKS
    others = range(1, ways)
    along = [lax.rem(t + d, ways) for d in range(ways)]

    def remote(src, dst, send, recv, where):
        return pltpu.make_async_remote_copy(
            src_ref=src, dst_ref=dst, send_sem=send, recv_sem=recv, device_id=where, device_id_type=MESH
        )

    own = [
        pltpu.make_async_copy(down_grads, keys.at[0, pl.ds(0, toks)], local_sem.at[0]),
        pltpu.make_async_copy(down_rows, tokens.at[pl.ds(0, toks)], local_sem.at[1]),
        pltpu.make_async_copy(weight.at[pl.ds(t * feats, feats)], rows.at[0], local_sem.at[2]),
    ]
    for copy in own:
        copy.start()

    barrier = pltpu.get_barrier_semaphore()

    def greet(where):
        pl.semaphore_signal(barrier, inc=1, device_id=where, device_id_type=MESH)

    for d in others:
        greet((s, along[d]))
    for d in range(ways):
        greet((mirror, along[d]))

    @pl.when(s < sections - 1)
    def _():
        greet((s + 1, t))

    has_next = s > 0
    is_own = after == s

    swaps = jnp.logical_and(has_next, jnp.logical_not(is_own))

    @pl.when(swaps)
    def _():
        greet((after, t))

    sent_to = 2 * ways - 1 + has_next.astype(jnp.int32) + swaps.astype(jnp.int32)
    pl.semaphore_wait(barrier, sent_to)

    mirror_key_copies = [
        remote(
            up_grads,
            keys.at[(ways - d) % ways, pl.ds(toks, toks)],
            mirror_key_send.at[d],
            mirror_key_recv.at[(ways - d) % ways],
            (mirror, along[d]),
        )
        for d in range(ways)
    ]
    key_copies = [
        remote(
            down_grads,
            keys.at[ways - d, pl.ds(0, toks)],
            key_send.at[d],
            key_recv.at[ways - d],
            (s, along[d]),
        )
        for d in others
    ]
    row_copies = [
        remote(
            up_rows.at[:, pl.ds(c * step, step)],
            tokens.at[pl.ds(toks, toks), pl.ds(c * step, step)],
            row_send.at[c],
            row_recv.at[c],
            (mirror, t),
        )
        for c in range(CHUNKS)
    ]
    weight_copies = [
        [
            remote(
                weight.at[pl.ds(along[d] * feats + c * step, step)],
                rows.at[ways - d, pl.ds(c * step, step)],
                weight_send.at[c, d],
                weight_recv.at[c, ways - d],
                (s, along[d]),
            )
            for d in others
        ]
        for c in range(CHUNKS)
    ]
    for copy in mirror_key_copies + key_copies + row_copies:
        copy.start()
    for copies in weight_copies:
        for copy in copies:
            copy.start()

    own[0].wait()
    own[1].wait()
    for copy in mirror_key_copies + key_copies:
        copy.wait_recv()
    grad_copies = []
    for c in range(CHUNKS):
        part = pl.ds(c * step, step)
        row_copies[c].wait_recv()
        all_keys = jnp.concatenate([keys[d] for d in range(ways)], axis=1)
        found = lax.dot_general(
            tokens[:, part], all_keys, (((0,), (0,)), ((), ())), preferred_element_type=jnp.float32
        ).astype(jnp.bfloat16)
        for d in range(ways):
            grads[d, part] = found[:, d * cols : (d + 1) * cols]
        for d in others:
            copy = remote(
                grads.at[d, part],
                grad_out.at[t, part],
                grad_send.at[c, d],
                grad_recv.at[c, ways - d],
                (s, along[d]),
            )
            copy.start()
            grad_copies.append(copy)
    own_grad = pltpu.make_async_copy(grads.at[0], grad_out.at[t], local_sem.at[3])
    own_grad.start()

    own[2].wait()

    def term_copies(c):
        part = pl.ds(c * step, step)
        down = remote(
            down_term.at[part], down_out.at[part], term_send.at[0, c], term_recv.at[0, c], (s - 1, t)
        )
        up = remote(
            up_term.at[part], up_out.at[part], term_send.at[1, c], term_recv.at[1, c], (after, t)
        )
        stay = pltpu.make_async_copy(up_term.at[part], up_out.at[part], term_send.at[1, c])
        return down, up, stay

    for c in range(CHUNKS):
        part = pl.ds(c * step, step)
        for copy in weight_copies[c]:
            copy.wait_recv()
        all_keys = jnp.concatenate([keys[d] for d in range(ways)], axis=1)
        all_rows = jnp.concatenate([rows[d, part] for d in range(ways)], axis=1)
        found = lax.dot_general(
            all_rows, all_keys, (((1,), (1,)), ((), ())), preferred_element_type=jnp.float32
        ).astype(jnp.bfloat16)
        down_term[part] = found[:, :toks]
        up_term[part] = found[:, toks:]
        down, up, stay = term_copies(c)

        @pl.when(has_next)
        def _():
            @pl.when(is_own)
            def _():
                stay.start()

            @pl.when(jnp.logical_not(is_own))
            def _():
                up.start()

            down.start()

    def clear(out, from_term):
        from_term[...] = jnp.zeros_like(from_term)
        fill = pltpu.make_async_copy(from_term, out, local_sem.at[4])
        fill.start()
        fill.wait()

    @pl.when(s == 0)
    def _():
        clear(up_out, up_term)

    for c in range(CHUNKS):
        down, up, stay = term_copies(c)

        @pl.when(s < sections - 1)
        def _():
            down.wait_recv()

        @pl.when(has_next)
        def _():
            @pl.when(is_own)
            def _():
                stay.wait()

            @pl.when(jnp.logical_not(is_own))
            def _():
                up.wait()

            down.wait_send()

    @pl.when(s == sections - 1)
    def _():
        clear(down_out, down_term)

    own_grad.wait()
    for copy in grad_copies:
        copy.wait()
    for copy in mirror_key_copies + key_copies + row_copies:
        copy.wait_send()
    for copies in weight_copies:
        for copy in copies:
            copy.wait_send()


def relay(sections, ways, weight, down_rows, up_rows, down_grads, up_grads):
    feats, toks, cols = down_rows.shape[1], down_rows.shape[0], down_grads.shape[1]
    dma = pltpu.SemaphoreType.DMA
    anywhere = pl.BlockSpec(memory_space=pl.ANY)
    return pl.pallas_call(
        lambda *refs: relay_kernel(sections, ways, *refs),
        out_shape=(
            jax.ShapeDtypeStruct((ways, feats, cols), jnp.bfloat16),
            jax.ShapeDtypeStruct((feats, toks), jnp.bfloat16),
            jax.ShapeDtypeStruct((feats, toks), jnp.bfloat16),
        ),
        in_specs=[anywhere] * 5,
        out_specs=(anywhere,) * 3,
        scratch_shapes=[
            pltpu.VMEM((2 * toks, feats), jnp.bfloat16),
            pltpu.VMEM((ways, 2 * toks, cols), jnp.bfloat16),
            pltpu.VMEM((ways, feats, cols), jnp.bfloat16),
            pltpu.VMEM((ways, feats, cols), jnp.bfloat16),
            pltpu.VMEM((feats, toks), jnp.bfloat16),
            pltpu.VMEM((feats, toks), jnp.bfloat16),
            dma((5,)),
            dma((ways,)),
            dma((ways,)),
            dma((ways,)),
            dma((ways,)),
            dma((CHUNKS,)),
            dma((CHUNKS,)),
            dma((CHUNKS, ways)),
            dma((CHUNKS, ways)),
            dma((CHUNKS, ways)),
            dma((CHUNKS, ways)),
            dma((2, CHUNKS)),
            dma((2, CHUNKS)),
        ],
        compiler_params=pltpu.CompilerParams(
            collective_id=0, has_side_effects=True, vmem_limit_bytes=60 * 1024 * 1024
        ),
    )(weight, down_rows, up_rows, down_grads, up_grads)


def local(
    key_weight, first_moment, second_moment, down_inputs, up_inputs, down_key_grads, up_key_grads
):
    weight = key_weight[0]
    gradient, down_received, up_received = relay(
        lax.axis_size("section"),
        lax.axis_size("tensor"),
        weight,
        down_inputs[0],
        up_inputs[0],
        down_key_grads[0],
        up_key_grads[0],
    )
    gradient = gradient.reshape(weight.shape).astype(jnp.float32)
    new_first = beta_one * first_moment[0] + (1.0 - beta_one) * gradient
    new_second = beta_two * second_moment[0] + (1.0 - beta_two) * gradient * gradient
    first_hat = new_first / (1.0 - beta_one**ADAM_STEP)
    second_hat = new_second / (1.0 - beta_two**ADAM_STEP)
    weight_full = weight.astype(jnp.float32)
    new_weight = weight_full - learn_rate * (
        first_hat / (jnp.sqrt(second_hat) + epsilon) + decay_rate * weight_full
    )
    return (
        new_weight[None],
        new_first[None],
        new_second[None],
        down_received[None],
        up_received[None],
    )


def solution(mesh):
    in_specs = (
        P("section", None, "tensor"),
        P("section", None, "tensor"),
        P("section", None, "tensor"),
        P("section", None, "tensor"),
        P("section", None, "tensor"),
        P("section", None, "tensor"),
        P("section", None, "tensor"),
    )
    out_specs = (
        P("section", None, "tensor"),
        P("section", None, "tensor"),
        P("section", None, "tensor"),
        P("section", "tensor", None),
        P("section", "tensor", None),
    )
    return jax.shard_map(local, mesh=mesh, in_specs=in_specs, out_specs=out_specs, check_vma=False)
```

time: 348 us -> 107 us (0.31)
  the two profiles are of different devices: /device:TPU:32 before, /device:TPU:31 now
where the time goes in v1:
time: 107 us
  Pallas kernels  98.2 us (92%)
  other arithmetic  6.36 us (6%)
  local copies, waits for them, and re-layouts  1.6 us (1%)
    pallas_call x1, Pallas kernels, relay(): pl.pallas_call(lambda *refs: relay_kernel(sections, ways, *refs), out_sha...  98.2 us
    sub x1, other arithmetic, local(): weight_full - learn_rate * (first_hat / (jnp.sqrt(second_hat) + epsilon)...  6.36 us

profile of v1, /device:TPU:31, one launch (start us, length us, event | category | flops | bytes accessed | tf_op | source)
XLA Modules:
  0.0 106.9 jit_solution(9446647910213611794)
XLA Ops:
  0.6 0.0 copy-start
  0.6 98.2 %shard_map.110 = (bf16[4,1024,128]{2,1,0:T(8,128)(2,1)}, bf16[1024,256]{1,0:T(8,128)(2,1)}, bf16[1024,256]{1,0:T(8,128)(2,1)}) custom-call(bf16[4096,128]{1,0:T(8,128)(2,1)} %bitcast.13, bf16[256,1024]{1,0:T(8,128)(2,1)} %bitcast.15, bf16[256,1024]{1,0:T(8,128)(2,1)} %bitcast.16, bf16[256,128]{1,0:T(8,128)(2,1)} %bitcast.19, bf16[256,128]{1,0:T(8,128)(2,1)} %bitcast.20), custom_call_target="tpu_custom_call" | custom-call | tf_op jit(solution)/shard_map/pallas_call | solution.py:263
  98.9 0.0 copy-done
  98.9 0.0 copy-start.2
  98.9 0.0 copy-start.1
  98.9 6.4 %convert_subtract_fusion = (f32[1,4096,128]{2,1,0:T(8,128)}, f32[1,4096,128]{2,1,0:T(8,128)}, f32[1,4096,128]{2,1,0:T(8,128)}) fusion(bf16[1,4096,128]{2,1,0:T(8,128)(2,1)S(1)} %copy-done, f32[1,4096,128]{2,1,0:T(8,128)} %param.8, f32[1,4096,128]{2,1,0:T(8,128)} %param.9, bf16[1,4096,128]{2,1,0:T(8,128)(2,1)} %bitcast.14), kind=kLoop, calls=%fused_computation.3 | loop fusion | flops 8912896 | bytes 12582912 | tf_op jit(solution)/shard_map/sub | solution.py:318
  105.3 0.0 copy-done.2
  105.3 0.8 copy.14
  106.1 0.0 copy-done.1
  106.1 0.8 copy.15
Async XLA Ops:
  0.6 98.3 %copy-start = (bf16[1,4096,128]{2,1,0:T(8,128)(2,1)S(1)}, bf16[1,4096,128]{2,1,0:T(8,128)(2,1)}, u32[]{:S(2)}) copy-start(bf16[1,4096,128]{2,1,0:T(8,128)(2,1)} %param.7) | copy-start | bytes 3145732
  98.9 6.4 %copy-start.2 = (bf16[1024,256]{1,0:T(8,128)(2,1)S(1)}, bf16[1024,256]{1,0:T(8,128)(2,1)}, u32[]{:S(2)}) copy-start(bf16[1024,256]{1,0:T(8,128)(2,1)} %get-tuple-element.9) | copy-start | bytes 1572868
  98.9 7.2 %copy-start.1 = (bf16[1024,256]{1,0:T(8,128)(2,1)S(1)}, bf16[1024,256]{1,0:T(8,128)(2,1)}, u32[]{:S(2)}) copy-start(bf16[1024,256]{1,0:T(8,128)(2,1)} %get-tuple-element.10) | copy-start | bytes 1572868

commit v2 on v1

v2 whole, which is shorter than its diff:
```python
import jax
import jax.numpy as jnp
from jax import lax
from jax.experimental import pallas as pl
from jax.experimental.pallas import tpu as pltpu
from jax.sharding import PartitionSpec as P

ADAM_STEP = 100


beta_one = 0.9
beta_two = 0.95
learn_rate = 0.00015
decay_rate = 0.1
epsilon = 1e-08

MESH = pl.DeviceIdType.MESH
CHUNKS = 4


def relay_kernel(
    sections,
    ways,
    weight,
    first_moment,
    second_moment,
    down_rows,
    up_rows,
    down_grads,
    up_grads,
    weight_out,
    first_out,
    second_out,
    down_out,
    up_out,
    own_weight,
    own_first,
    own_second,
    tokens,
    keys,
    rows,
    grads,
    arrived,
    down_term,
    up_term,
    passing,
    local_sem,
    key_send,
    key_recv,
    row_send,
    row_recv,
    weight_send,
    weight_recv,
    grad_send,
    grad_recv,
    term_send,
    term_recv,
    pass_recv,
):
    s = lax.axis_index("section")
    t = lax.axis_index("tensor")
    mirror = sections - 1 - s
    after = sections - s
    half = sections // 2
    toks, feats = down_rows.shape
    cols = down_grads.shape[1]
    step = feats // CHUNKS
    others = range(1, ways)
    back = ways - 1
    far = ways // 2
    along = [lax.rem(t + d, ways) for d in range(ways)]
    down_part, up_part = pl.ds(0, toks), pl.ds(toks, toks)

    def remote(src, dst, send, recv, where):
        return pltpu.make_async_remote_copy(
            src_ref=src, dst_ref=dst, send_sem=send, recv_sem=recv, device_id=where, device_id_type=MESH
        )

    barrier = pltpu.get_barrier_semaphore()

    def greet(where):
        pl.semaphore_signal(barrier, inc=1, device_id=where, device_id_type=MESH)

    for d in others:
        greet((s, along[d]))
    greet((mirror, t))

    first, last, middle = s == 0, s == sections - 1, s == half
    joint = s == half - 1

    @pl.when(jnp.logical_not(jnp.logical_or(last, joint)))
    def _():
        greet((s + 1, t))

    @pl.when(joint)
    def _():
        greet((0, t))

    @pl.when(first)
    def _():
        greet((half, t))

    swaps = jnp.logical_not(jnp.logical_or(first, middle))

    @pl.when(swaps)
    def _():
        greet((after, t))

    own = [
        pltpu.make_async_copy(down_grads, keys.at[0, down_part], local_sem.at[0]),
        pltpu.make_async_copy(down_rows, tokens.at[down_part], local_sem.at[1]),
    ]
    for d in range(ways):
        block = pl.ds(along[d] * feats, feats)
        own += [
            pltpu.make_async_copy(weight.at[block], own_weight.at[d], local_sem.at[2 + 3 * d]),
            pltpu.make_async_copy(first_moment.at[block], own_first.at[d], local_sem.at[3 + 3 * d]),
            pltpu.make_async_copy(second_moment.at[block], own_second.at[d], local_sem.at[4 + 3 * d]),
        ]
    for copy in own:
        copy.start()

    pl.semaphore_wait(barrier, ways + 1 + swaps.astype(jnp.int32))

    to_mirror = remote(up_grads, keys.at[0, up_part], key_send.at[0], key_recv.at[0], (mirror, t))
    down_keys = {
        1: remote(down_grads, keys.at[back, down_part], key_send.at[1], key_recv.at[1], (s, along[1])),
        back: remote(down_grads, keys.at[1, down_part], key_send.at[2], key_recv.at[2], (s, along[back])),
    }
    up_keys = {
        1: remote(keys.at[0, up_part], keys.at[back, up_part], key_send.at[3], key_recv.at[3], (s, along[1])),
        back: remote(keys.at[0, up_part], keys.at[1, up_part], key_send.at[4], key_recv.at[4], (s, along[back])),
    }
    far_down = remote(
        keys.at[back, down_part], keys.at[far, down_part], key_send.at[5], key_recv.at[5], (s, along[1])
    )
    far_up = remote(
        keys.at[1, up_part], keys.at[far, up_part], key_send.at[6], key_recv.at[6], (s, along[back])
    )
    row_copies = [
        remote(
            up_rows.at[:, pl.ds(c * step, step)],
            tokens.at[up_part, pl.ds(c * step, step)],
            row_send.at[c],
            row_recv.at[c],
            (mirror, t),
        )
        for c in range(CHUNKS)
    ]
    weight_copies = [
        [
            remote(
                weight.at[pl.ds(along[d] * feats + c * step, step)],
                rows.at[ways - d, pl.ds(c * step, step)],
                weight_send.at[c, d],
                weight_recv.at[c, ways - d],
                (s, along[d]),
            )
            for d in others
        ]
        for c in range(CHUNKS)
    ]
    to_mirror.start()
    down_keys[1].start()
    down_keys[back].start()
    for copy in weight_copies[0]:
        copy.start()
    to_mirror.wait_recv()
    up_keys[1].start()
    up_keys[back].start()
    down_keys[1].wait_recv()
    far_down.start()
    up_keys[back].wait_recv()
    far_up.start()
    for copies in weight_copies[1:]:
        for copy in copies:
            copy.start()
    for copy in row_copies:
        copy.start()
    for copy in own:
        copy.wait()
    for copy in (down_keys[back], up_keys[1], far_down, far_up):
        copy.wait_recv()

    def down_copy(c):
        part = pl.ds(c * step, step)
        return remote(
            down_term.at[part], down_out.at[part], term_send.at[0, c], term_recv.at[0, c], (s - 1, t)
        )

    def first_leg(c):
        part = pl.ds(c * step, step)
        return remote(down_term.at[part], passing.at[part], term_send.at[0, c], pass_recv.at[c], (0, t))

    def second_leg(c):
        part = pl.ds(c * step, step)
        return remote(
            passing.at[part], down_out.at[part], term_send.at[0, c], term_recv.at[0, c], (half - 1, t)
        )

    def up_copy(c):
        part = pl.ds(c * step, step)
        return remote(
            up_term.at[part], up_out.at[part], term_send.at[1, c], term_recv.at[1, c], (after, t)
        )

    sends_on = jnp.logical_not(jnp.logical_or(first, middle))

    for c in range(CHUNKS):
        part = pl.ds(c * step, step)
        for copy in weight_copies[c]:
            copy.wait_recv()
        all_keys = jnp.concatenate([keys[d] for d in range(ways)], axis=1)
        all_rows = jnp.concatenate(
            [own_weight[0, part]] + [rows[d, part] for d in others], axis=1
        )
        found = lax.dot_general(
            all_rows, all_keys, (((1,), (1,)), ((), ())), preferred_element_type=jnp.float32
        ).astype(jnp.bfloat16)
        down_term[part] = found[:, :toks]
        up_term[part] = found[:, toks:]

        @pl.when(sends_on)
        def _():
            up_copy(c).start()
            down_copy(c).start()

        @pl.when(middle)
        def _():
            first_leg(c).start()
            up_out[part] = found[:, toks:]

    def grad_copies(c):
        part = pl.ds(c * step, step)
        return [
            remote(
                grads.at[d, part],
                arrived.at[ways - d, part],
                grad_send.at[c, d],
                grad_recv.at[c, ways - d],
                (s, along[d]),
            )
            for d in others
        ]

    for c in range(CHUNKS):
        part = pl.ds(c * step, step)
        row_copies[c].wait_recv()
        all_keys = jnp.concatenate([keys[d] for d in range(ways)], axis=1)
        found = lax.dot_general(
            tokens[:, part], all_keys, (((0,), (0,)), ((), ())), preferred_element_type=jnp.float32
        ).astype(jnp.bfloat16)
        for d in range(ways):
            grads[d, part] = found[:, d * cols : (d + 1) * cols]
        for copy in grad_copies(c):
            copy.start()

    @pl.when(first)
    def _():
        for c in range(CHUNKS):
            first_leg(c).wait_recv()
            second_leg(c).start()

    @pl.when(first)
    def _():
        up_out[...] = jnp.zeros_like(up_out)

    @pl.when(last)
    def _():
        down_out[...] = jnp.zeros_like(down_out)

    def update(d, c, gradient):
        part = pl.ds(c * step, step)
        here = pl.ds(pl.multiple_of(along[d] * feats + c * step, step), step)
        gradient = gradient.astype(jnp.float32)
        new_first = beta_one * own_first[d, part] + (1.0 - beta_one) * gradient
        new_second = beta_two * own_second[d, part] + (1.0 - beta_two) * gradient * gradient
        first_hat = new_first * (1.0 / (1.0 - beta_one**ADAM_STEP))
        second_hat = new_second * (1.0 / (1.0 - beta_two**ADAM_STEP))
        held = own_weight[d, part].astype(jnp.float32)
        first_out[here] = new_first
        second_out[here] = new_second
        weight_out[here] = held - learn_rate * (
            first_hat / (jnp.sqrt(second_hat) + epsilon) + decay_rate * held
        )

    for c in range(CHUNKS):
        update(0, c, grads[0, pl.ds(c * step, step)])

    for c in range(CHUNKS):
        for copy, d in zip(grad_copies(c), others):
            copy.wait_recv()
            update(ways - d, c, arrived[ways - d, pl.ds(c * step, step)])

    for c in range(CHUNKS):
        @pl.when(jnp.logical_not(last))
        def _():
            down_copy(c).wait_recv()

        @pl.when(swaps)
        def _():
            up_copy(c).wait_recv()

    for c in range(CHUNKS):
        for copy in grad_copies(c) + weight_copies[c]:
            copy.wait_send()

        down_copy(c).wait_send()

        @pl.when(swaps)
        def _():
            up_copy(c).wait_send()

    for copy in [to_mirror, *down_keys.values(), *up_keys.values(), far_down, far_up, *row_copies]:
        copy.wait_send()


def relay(sections, ways, weight, first_moment, second_moment, down_rows, up_rows, down_grads, up_grads):
    feats, toks, cols = down_rows.shape[1], down_rows.shape[0], down_grads.shape[1]
    dma = pltpu.SemaphoreType.DMA
    state = pltpu.VMEM(weight.shape, jnp.float32)
    term = pltpu.VMEM((feats, toks), jnp.bfloat16)
    block = (ways, feats, cols)
    operands = [
        pltpu.with_memory_space_constraint(x, pltpu.HBM)
        for x in (weight, first_moment, second_moment, down_rows, up_rows, down_grads, up_grads)
    ]
    return pl.pallas_call(
        lambda *refs: relay_kernel(sections, ways, *refs),
        out_shape=(state, state, state, term, term),
        in_specs=[pl.BlockSpec(memory_space=pltpu.HBM)] * 7,
        out_specs=(pl.BlockSpec(memory_space=pltpu.VMEM),) * 5,
        scratch_shapes=[
            pltpu.VMEM(block, jnp.bfloat16),
            pltpu.VMEM(block, jnp.float32),
            pltpu.VMEM(block, jnp.float32),
            pltpu.VMEM((2 * toks, feats), jnp.bfloat16),
            pltpu.VMEM((ways, 2 * toks, cols), jnp.bfloat16),
            pltpu.VMEM(block, jnp.bfloat16),
            pltpu.VMEM(block, jnp.bfloat16),
            pltpu.VMEM(block, jnp.bfloat16),
            pltpu.VMEM((feats, toks), jnp.bfloat16),
            pltpu.VMEM((feats, toks), jnp.bfloat16),
            pltpu.VMEM((feats, toks), jnp.bfloat16),
            dma((2 + 3 * ways,)),
            dma((7,)),
            dma((7,)),
            dma((CHUNKS,)),
            dma((CHUNKS,)),
            dma((CHUNKS, ways)),
            dma((CHUNKS, ways)),
            dma((CHUNKS, ways)),
            dma((CHUNKS, ways)),
            dma((2, CHUNKS)),
            dma((2, CHUNKS)),
            dma((CHUNKS,)),
        ],
        compiler_params=pltpu.CompilerParams(
            collective_id=0, has_side_effects=True, vmem_limit_bytes=16 * 1024 * 1024
        ),
    )(*operands)


def leave_kernel(*refs):
    count = len(refs) // 2
    sems = refs[-1]
    copies = [
        pltpu.make_async_copy(refs[i], refs[count + i], sems.at[i]) for i in range(count)
    ]
    for copy in copies:
        copy.start()
    for copy in copies:
        copy.wait()


def leave(*arrays):
    return pl.pallas_call(
        leave_kernel,
        out_shape=tuple(jax.ShapeDtypeStruct(x.shape, x.dtype) for x in arrays),
        in_specs=[pl.BlockSpec(memory_space=pltpu.VMEM)] * len(arrays),
        out_specs=(pl.BlockSpec(memory_space=pl.ANY),) * len(arrays),
        scratch_shapes=[pltpu.SemaphoreType.DMA((len(arrays),))],
        compiler_params=pltpu.CompilerParams(vmem_limit_bytes=16 * 1024 * 1024),
    )(*(pltpu.with_memory_space_constraint(x, pltpu.VMEM) for x in arrays))


def local(
    key_weight, first_moment, second_moment, down_inputs, up_inputs, down_key_grads, up_key_grads
):
    arrays = relay(
        lax.axis_size("section"),
        lax.axis_size("tensor"),
        key_weight[0],
        first_moment[0],
        second_moment[0],
        down_inputs[0],
        up_inputs[0],
        down_key_grads[0],
        up_key_grads[0],
    )
    return tuple(x[None] for x in leave(*arrays))


def solution(mesh):
    in_specs = (
        P("section", None, "tensor"),
        P("section", None, "tensor"),
        P("section", None, "tensor"),
        P("section", None, "tensor"),
        P("section", None, "tensor"),
        P("section", None, "tensor"),
        P("section", None, "tensor"),
    )
    out_specs = (
        P("section", None, "tensor"),
        P("section", None, "tensor"),
        P("section", None, "tensor"),
        P("section", "tensor", None),
        P("section", "tensor", None),
    )
    return jax.shard_map(local, mesh=mesh, in_specs=in_specs, out_specs=out_specs, check_vma=False)
```

time: 107 us -> 96.6 us (0.903)
  the two profiles are of different devices: /device:TPU:31 before, /device:TPU:32 now
where the time goes in v2:
time: 96.6 us; the launch traced here: 95.8 us
  Pallas kernels  95.1 us (98%)
    pallas_call x1, Pallas kernels, relay(): pl.pallas_call(lambda *refs: relay_kernel(sections, ways, *refs), out_sha...  92.1 us
    pallas_call x1, Pallas kernels, leave(): pl.pallas_call(leave_kernel, out_shape=tuple((jax.ShapeDtypeStruct(x.shap...  3.01 us

profile of v2, /device:TPU:32, one launch (start us, length us, event | category | flops | bytes accessed | tf_op | source)
XLA Modules:
  0.0 95.8 jit_solution(6650404567930403521)
XLA Ops:
  0.6 92.1 %shard_map.110 = (f32[4096,128]{1,0:T(8,128)S(1)}, f32[4096,128]{1,0:T(8,128)S(1)}, f32[4096,128]{1,0:T(8,128)S(1)}, bf16[1024,256]{1,0:T(8,128)(2,1)S(1)}, bf16[1024,256]{1,0:T(8,128)(2,1)S(1)}) custom-call(bf16[4096,128]{1,0:T(8,128)(2,1)} %bitcast.14, f32[4096,128]{1,0:T(8,128)} %bitcast.12, f32[4096,128]{1,0:T(8,128)} %bitcast.13, ...), custom_call_target="tpu_custom_call" | custom-call | tf_op jit(solution)/shard_map/pallas_call | solution.py:328
  92.8 3.0 %shard_map.111 = (f32[4096,128]{1,0:T(8,128)}, f32[4096,128]{1,0:T(8,128)}, f32[4096,128]{1,0:T(8,128)}, bf16[1024,256]{1,0:T(8,128)(2,1)}, bf16[1024,256]{1,0:T(8,128)(2,1)}) custom-call(f32[4096,128]{1,0:T(8,128)S(1)} %get-tuple-element.15.refs_0_, f32[4096,128]{1,0:T(8,128)S(1)} %get-tuple-element.16.refs_1_, f32[4096,128]{1,0:T(8,128)S(1)} %get-tuple-element.17.refs_2_, ...), custom_call_target="tpu_custom_call" | custom-call | tf_op jit(solution)/shard_map/pallas_call | solution.py:377

commit v3 on v2

--- a/solution.py
+++ b/solution.py
@@ -84,6 +84,7 @@
     for d in others:
         greet((s, along[d]))
     greet((mirror, t))
+    greet((mirror, lax.rem(t + jnp.where(s < half, back, 1), ways)))
 
     first, last, middle = s == 0, s == sections - 1, s == half
     joint = s == half - 1
@@ -120,23 +121,19 @@
     for copy in own:
         copy.start()
 
-    pl.semaphore_wait(barrier, ways + 1 + swaps.astype(jnp.int32))
-
+    pl.semaphore_wait(barrier, ways + 2 + swaps.astype(jnp.int32))
+
+    turn = jnp.where(s < half, 1, back)
+    other = ways - turn
+    ahead, behind = (s, lax.rem(t + turn, ways)), (s, lax.rem(t + other, ways))
     to_mirror = remote(up_grads, keys.at[0, up_part], key_send.at[0], key_recv.at[0], (mirror, t))
-    down_keys = {
-        1: remote(down_grads, keys.at[back, down_part], key_send.at[1], key_recv.at[1], (s, along[1])),
-        back: remote(down_grads, keys.at[1, down_part], key_send.at[2], key_recv.at[2], (s, along[back])),
-    }
-    up_keys = {
-        1: remote(keys.at[0, up_part], keys.at[back, up_part], key_send.at[3], key_recv.at[3], (s, along[1])),
-        back: remote(keys.at[0, up_part], keys.at[1, up_part], key_send.at[4], key_recv.at[4], (s, along[back])),
-    }
-    far_down = remote(
-        keys.at[back, down_part], keys.at[far, down_part], key_send.at[5], key_recv.at[5], (s, along[1])
+    to_side = remote(
+        up_grads, keys.at[turn, up_part], key_send.at[1], key_recv.at[1], (mirror, lax.rem(t + other, ways))
     )
-    far_up = remote(
-        keys.at[1, up_part], keys.at[far, up_part], key_send.at[6], key_recv.at[6], (s, along[back])
-    )
+    down_ahead = remote(down_grads, keys.at[other, down_part], key_send.at[2], key_recv.at[2], ahead)
+    down_behind = remote(down_grads, keys.at[turn, down_part], key_send.at[3], key_recv.at[3], behind)
+    up_behind = remote(keys.at[0, up_part], keys.at[turn, up_part], key_send.at[4], key_recv.at[4], behind)
+    both_far = remote(keys.at[other], keys.at[far], key_send.at[5], key_recv.at[5], ahead)
     row_copies = [
         remote(
             up_rows.at[:, pl.ds(c * step, step)],
@@ -160,18 +157,15 @@
         ]
         for c in range(CHUNKS)
     ]
-    to_mirror.start()
-    down_keys[1].start()
-    down_keys[back].start()
+    for copy in (to_mirror, to_side, down_ahead, down_behind):
+        copy.start()
     for copy in weight_copies[0]:
         copy.start()
     to_mirror.wait_recv()
-    up_keys[1].start()
-    up_keys[back].start()
-    down_keys[1].wait_recv()
-    far_down.start()
-    up_keys[back].wait_recv()
-    far_up.start()
+    up_behind.start()
+    to_side.wait_recv()
+    down_ahead.wait_recv()
+    both_far.start()
     for copies in weight_copies[1:]:
         for copy in copies:
             copy.start()
@@ -179,7 +173,7 @@
         copy.start()
     for copy in own:
         copy.wait()
-    for copy in (down_keys[back], up_keys[1], far_down, far_up):
+    for copy in (down_behind, up_behind, both_far):
         copy.wait_recv()
 
     def down_copy(c):
@@ -206,7 +200,7 @@
 
     sends_on = jnp.logical_not(jnp.logical_or(first, middle))
 
-    for c in range(CHUNKS):
+    def make_terms(c):
         part = pl.ds(c * step, step)
         for copy in weight_copies[c]:
             copy.wait_recv()
@@ -223,12 +217,12 @@
         @pl.when(sends_on)
         def _():
             up_copy(c).start()
-            down_copy(c).start()
 
         @pl.when(middle)
         def _():
             first_leg(c).start()
             up_out[part] = found[:, toks:]
+
 
     def grad_copies(c):
         part = pl.ds(c * step, step)
@@ -243,7 +237,22 @@
             for d in others
         ]
 
-    for c in range(CHUNKS):
+    def send_grads(c, low, high):
+        part = pl.ds(c * step, step)
+        for there in range(low, high):
+            d = lax.rem(there + ways - t, ways)
+
+            @pl.when(d != 0)
+            def _():
+                remote(
+                    grads.at[d, part],
+                    arrived.at[ways - d, part],
+                    grad_send.at[c, d],
+                    grad_recv.at[c, ways - d],
+                    (s, there),
+                ).start()
+
+    def make_grads(c):
         part = pl.ds(c * step, step)
         row_copies[c].wait_recv()
         all_keys = jnp.concatenate([keys[d] for d in range(ways)], axis=1)
@@ -252,8 +261,28 @@
         ).astype(jnp.bfloat16)
         for d in range(ways):
             grads[d, part] = found[:, d * cols : (d + 1) * cols]
-        for copy in grad_copies(c):
-            copy.start()
+
+    make_terms(0)
+    make_terms(1)
+    make_grads(0)
+    send_grads(0, 0, far)
+    make_terms(2)
+    make_grads(1)
+    send_grads(1, 0, far)
+    send_grads(0, far, ways)
+    make_terms(3)
+    make_grads(2)
+    send_grads(2, 0, far)
+    send_grads(1, far, ways)
+    make_grads(3)
+    send_grads(3, 0, far)
+    send_grads(2, far, ways)
+    send_grads(3, far, ways)
+
+    @pl.when(sends_on)
+    def _():
+        for c in range(CHUNKS):
+            down_copy(c).start()
 
     @pl.when(first)
     def _():
@@ -311,7 +340,7 @@
         def _():
             up_copy(c).wait_send()
 
-    for copy in [to_mirror, *down_keys.values(), *up_keys.values(), far_down, far_up, *row_copies]:
+    for copy in [to_mirror, to_side, down_ahead, down_behind, up_behind, both_far, *row_copies]:
         copy.wait_send()
 
 
@@ -343,8 +372,8 @@
             pltpu.VMEM((feats, toks), jnp.bfloat16),
             pltpu.VMEM((feats, toks), jnp.bfloat16),
             dma((2 + 3 * ways,)),
-            dma((7,)),
-            dma((7,)),
+            dma((6,)),
+            dma((6,)),
             dma((CHUNKS,)),
             dma((CHUNKS,)),
             dma((CHUNKS, ways)),

time: 96.6 us -> 93 us (0.963)
  Pallas kernels: 95.1 us -> 92.2 us
    pallas_call x1, Pallas kernels: 92.1 us -> 89.2 us  [relay(): pl.pallas_call(lambda *refs: relay_kernel(sections, ways, *refs), out_sha...]
where the time goes in v3:
time: 93 us; the launch traced here: 92.9 us
  Pallas kernels  92.2 us (99%)
    pallas_call x1, Pallas kernels, relay(): pl.pallas_call(lambda *refs: relay_kernel(sections, ways, *refs), out_sha...  89.2 us
    pallas_call x1, Pallas kernels, leave(): pl.pallas_call(leave_kernel, out_shape=tuple((jax.ShapeDtypeStruct(x.shap...  3.01 us

profile of v3, /device:TPU:32, one launch (start us, length us, event | category | flops | bytes accessed | tf_op | source)
XLA Modules:
  0.0 92.9 jit_solution(1502381917397848516)
XLA Ops:
  0.6 89.2 %shard_map.110 = (f32[4096,128]{1,0:T(8,128)S(1)}, f32[4096,128]{1,0:T(8,128)S(1)}, f32[4096,128]{1,0:T(8,128)S(1)}, bf16[1024,256]{1,0:T(8,128)(2,1)S(1)}, bf16[1024,256]{1,0:T(8,128)(2,1)S(1)}) custom-call(bf16[4096,128]{1,0:T(8,128)(2,1)} %bitcast.14, f32[4096,128]{1,0:T(8,128)} %bitcast.12, f32[4096,128]{1,0:T(8,128)} %bitcast.13, ...), custom_call_target="tpu_custom_call" | custom-call | tf_op jit(solution)/shard_map/pallas_call | solution.py:357
  89.9 3.0 %shard_map.111 = (f32[4096,128]{1,0:T(8,128)}, f32[4096,128]{1,0:T(8,128)}, f32[4096,128]{1,0:T(8,128)}, bf16[1024,256]{1,0:T(8,128)(2,1)}, bf16[1024,256]{1,0:T(8,128)(2,1)}) custom-call(f32[4096,128]{1,0:T(8,128)S(1)} %get-tuple-element.15.refs_0_, f32[4096,128]{1,0:T(8,128)S(1)} %get-tuple-element.16.refs_1_, f32[4096,128]{1,0:T(8,128)S(1)} %get-tuple-element.17.refs_2_, ...), custom_call_target="tpu_custom_call" | custom-call | tf_op jit(solution)/shard_map/pallas_call | solution.py:406

commit v4 on v3

--- a/solution.py
+++ b/solution.py
@@ -16,6 +16,8 @@
 
 MESH = pl.DeviceIdType.MESH
 CHUNKS = 4
+EARLY = 2
+RELAYED = 3
 
 
 def relay_kernel(
@@ -44,6 +46,7 @@
     down_term,
     up_term,
     passing,
+    ready,
     local_sem,
     key_send,
     key_recv,
@@ -81,10 +84,15 @@
     def greet(where):
         pl.semaphore_signal(barrier, inc=1, device_id=where, device_id_type=MESH)
 
-    for d in others:
-        greet((s, along[d]))
+    late = t >= far
+    side = lax.rem(t + jnp.where(s < half, back, 1), ways)
+    peers = [(s, along[d]) for d in others] + [(mirror, side)]
     greet((mirror, t))
-    greet((mirror, lax.rem(t + jnp.where(s < half, back, 1), ways)))
+    for peer in peers:
+
+        @pl.when(jnp.logical_not(jnp.logical_and(late, peer[1] < far)))
+        def _():
+            greet(peer)
 
     first, last, middle = s == 0, s == sections - 1, s == half
     joint = s == half - 1
@@ -96,6 +104,7 @@
     @pl.when(joint)
     def _():
         greet((0, t))
+        greet((half, t))
 
     @pl.when(first)
     def _():
@@ -121,7 +130,15 @@
     for copy in own:
         copy.start()
 
-    pl.semaphore_wait(barrier, ways + 2 + swaps.astype(jnp.int32))
+    side_late = (side >= far).astype(jnp.int32)
+    later = jnp.where(late, 0, ways - far + side_late)
+    pl.semaphore_wait(barrier, ways + 2 + (swaps | middle).astype(jnp.int32) - later)
+
+    for peer in peers:
+
+        @pl.when(jnp.logical_and(late, peer[1] < far))
+        def _():
+            pl.semaphore_signal(ready, inc=1, device_id=peer, device_id_type=MESH)
 
     turn = jnp.where(s < half, 1, back)
     other = ways - turn
@@ -144,33 +161,42 @@
         )
         for c in range(CHUNKS)
     ]
-    weight_copies = [
-        [
-            remote(
-                weight.at[pl.ds(along[d] * feats + c * step, step)],
-                rows.at[ways - d, pl.ds(c * step, step)],
-                weight_send.at[c, d],
-                weight_recv.at[c, ways - d],
-                (s, along[d]),
-            )
-            for d in others
-        ]
-        for c in range(CHUNKS)
-    ]
-    for copy in (to_mirror, to_side, down_ahead, down_behind):
+    def weight_copy(c, d):
+        there = lax.rem(t + d, ways)
+        return remote(
+            weight.at[pl.ds(there * feats + c * step, step)],
+            rows.at[ways - d, pl.ds(c * step, step)],
+            weight_send.at[c, d],
+            weight_recv.at[c, ways - d],
+            (s, there),
+        )
+
+    weight_copies = [[weight_copy(c, d) for d in others] for c in range(CHUNKS)]
+    near = jnp.where(lax.rem(t, 2) == 0, 1, back)
+
+    to_mirror.start()
+    for copy in row_copies:
         copy.start()
-    for copy in weight_copies[0]:
+    for c in range(EARLY):
+        weight_copy(c, near).start()
+
+    @pl.when(jnp.logical_not(late))
+    def _():
+        pl.semaphore_wait(ready, ways - far + side_late)
+
+    for copy in (to_side, down_ahead, down_behind):
         copy.start()
+    for c in range(EARLY):
+        weight_copy(c, far).start()
+        weight_copy(c, ways - near).start()
     to_mirror.wait_recv()
     up_behind.start()
     to_side.wait_recv()
     down_ahead.wait_recv()
     both_far.start()
-    for copies in weight_copies[1:]:
+    for copies in weight_copies[EARLY:]:
         for copy in copies:
             copy.start()
-    for copy in row_copies:
-        copy.start()
     for copy in own:
         copy.wait()
     for copy in (down_behind, up_behind, both_far):
@@ -185,6 +211,12 @@
     def first_leg(c):
         part = pl.ds(c * step, step)
         return remote(down_term.at[part], passing.at[part], term_send.at[0, c], pass_recv.at[c], (0, t))
+
+    def direct(c):
+        part = pl.ds(c * step, step)
+        return remote(
+            down_term.at[part], down_out.at[part], term_send.at[0, c], term_recv.at[0, c], (half - 1, t)
+        )
 
     def second_leg(c):
         part = pl.ds(c * step, step)
@@ -220,7 +252,7 @@
 
         @pl.when(middle)
         def _():
-            first_leg(c).start()
+            (first_leg(c) if c < RELAYED else direct(c)).start()
             up_out[part] = found[:, toks:]
 
 
@@ -262,22 +294,102 @@
         for d in range(ways):
             grads[d, part] = found[:, d * cols : (d + 1) * cols]
 
-    make_terms(0)
-    make_terms(1)
-    make_grads(0)
-    send_grads(0, 0, far)
-    make_terms(2)
-    make_grads(1)
-    send_grads(1, 0, far)
-    send_grads(0, far, ways)
-    make_terms(3)
-    make_grads(2)
-    send_grads(2, 0, far)
-    send_grads(1, far, ways)
-    make_grads(3)
-    send_grads(3, 0, far)
-    send_grads(2, far, ways)
-    send_grads(3, far, ways)
+    ends = jnp.logical_or(first, middle)
+    early_rest = jnp.logical_and(t < far, jnp.logical_not(ends))
+    late_rest = jnp.logical_and(t >= far, jnp.logical_not(ends))
+    early_middle = jnp.logical_and(t < far, middle)
+    late_middle = jnp.logical_and(t >= far, middle)
+
+    @pl.when(early_rest)
+    def _():
+        make_terms(0)
+        make_terms(1)
+        make_grads(0)
+        send_grads(0, 0, far)
+        make_terms(2)
+        make_grads(1)
+        send_grads(1, 0, far)
+        send_grads(0, far, ways)
+        make_terms(3)
+        make_grads(2)
+        send_grads(2, 0, far)
+        send_grads(1, far, ways)
+        make_grads(3)
+        send_grads(3, 0, far)
+        send_grads(2, far, ways)
+        send_grads(3, far, ways)
+
+    @pl.when(late_rest)
+    def _():
+        make_grads(0)
+        send_grads(0, 0, far)
+        make_grads(1)
+        send_grads(1, 0, far)
+        make_grads(2)
+        send_grads(2, 0, far)
+        make_grads(3)
+        send_grads(3, 0, far)
+        make_terms(0)
+        send_grads(0, far, ways)
+        make_terms(1)
+        send_grads(1, far, ways)
+        make_terms(2)
+        send_grads(2, far, ways)
+        make_terms(3)
+        send_grads(3, far, ways)
+
+    @pl.when(early_middle)
+    def _():
+        make_grads(0)
+        send_grads(0, 0, far)
+        make_grads(1)
+        send_grads(1, 0, far)
+        make_grads(2)
+        send_grads(2, 0, far)
+        make_grads(3)
+        send_grads(3, 0, far)
+        make_terms(0)
+        make_terms(1)
+        make_terms(2)
+        make_terms(3)
+        send_grads(0, far, ways)
+        send_grads(1, far, ways)
+        send_grads(2, far, ways)
+        send_grads(3, far, ways)
+
+    @pl.when(late_middle)
+    def _():
+        make_terms(0)
+        make_terms(1)
+        make_terms(2)
+        make_grads(0)
+        send_grads(0, 0, far)
+        make_grads(1)
+        send_grads(1, 0, far)
+        make_grads(2)
+        send_grads(2, 0, far)
+        make_grads(3)
+        send_grads(3, 0, far)
+        make_terms(3)
+        send_grads(0, far, ways)
+        send_grads(1, far, ways)
+        send_grads(2, far, ways)
+        send_grads(3, far, ways)
+
+    @pl.when(first)
+    def _():
+        make_grads(0)
+        send_grads(0, 0, far)
+        make_grads(1)
+        send_grads(1, 0, far)
+        make_grads(2)
+        send_grads(2, 0, far)
+        make_grads(3)
+        send_grads(3, 0, far)
+        send_grads(0, far, ways)
+        send_grads(1, far, ways)
+        send_grads(2, far, ways)
+        send_grads(3, far, ways)
 
     @pl.when(sends_on)
     def _():
@@ -286,9 +398,12 @@
 
     @pl.when(first)
     def _():
-        for c in range(CHUNKS):
+        for c in range(RELAYED):
             first_leg(c).wait_recv()
             second_leg(c).start()
+        for copies in weight_copies:
+            for copy in copies:
+                copy.wait_recv()
 
     @pl.when(first)
     def _():
@@ -334,7 +449,9 @@
         for copy in grad_copies(c) + weight_copies[c]:
             copy.wait_send()
 
-        down_copy(c).wait_send()
+        @pl.when(jnp.logical_or(jnp.logical_not(first), c < RELAYED))
+        def _():
+            down_copy(c).wait_send()
 
         @pl.when(swaps)
         def _():
@@ -371,6 +488,7 @@
             pltpu.VMEM((feats, toks), jnp.bfloat16),
             pltpu.VMEM((feats, toks), jnp.bfloat16),
             pltpu.VMEM((feats, toks), jnp.bfloat16),
+            pltpu.SemaphoreType.REGULAR,
             dma((2 + 3 * ways,)),
             dma((6,)),
             dma((6,)),

time: 93 us -> 91.6 us (0.985)
  Pallas kernels: 92.2 us -> 90.9 us
    pallas_call x1, Pallas kernels: 89.2 us -> 87.9 us  [relay(): pl.pallas_call(lambda *refs: relay_kernel(sections, ways, *refs), out_sha...]
where the time goes in v4:
time: 91.6 us; the launch traced here: 91.5 us
  Pallas kernels  90.9 us (99%)
    pallas_call x1, Pallas kernels, relay(): pl.pallas_call(lambda *refs: relay_kernel(sections, ways, *refs), out_sha...  87.9 us
    pallas_call x1, Pallas kernels, leave(): pl.pallas_call(leave_kernel, out_shape=tuple((jax.ShapeDtypeStruct(x.shap...  3.01 us

profile of v4, /device:TPU:32, one launch (start us, length us, event | category | flops | bytes accessed | tf_op | source)
XLA Modules:
  0.0 91.5 jit_solution(14170187552362273267)
XLA Ops:
  0.6 87.9 %shard_map.110 = (f32[4096,128]{1,0:T(8,128)S(1)}, f32[4096,128]{1,0:T(8,128)S(1)}, f32[4096,128]{1,0:T(8,128)S(1)}, bf16[1024,256]{1,0:T(8,128)(2,1)S(1)}, bf16[1024,256]{1,0:T(8,128)(2,1)S(1)}) custom-call(bf16[4096,128]{1,0:T(8,128)(2,1)} %bitcast.14, f32[4096,128]{1,0:T(8,128)} %bitcast.12, f32[4096,128]{1,0:T(8,128)} %bitcast.13, ...), custom_call_target="tpu_custom_call" | custom-call | tf_op jit(solution)/shard_map/pallas_call | solution.py:474
  88.5 3.0 %shard_map.111 = (f32[4096,128]{1,0:T(8,128)}, f32[4096,128]{1,0:T(8,128)}, f32[4096,128]{1,0:T(8,128)}, bf16[1024,256]{1,0:T(8,128)(2,1)}, bf16[1024,256]{1,0:T(8,128)(2,1)}) custom-call(f32[4096,128]{1,0:T(8,128)S(1)} %get-tuple-element.15.refs_0_, f32[4096,128]{1,0:T(8,128)S(1)} %get-tuple-element.16.refs_1_, f32[4096,128]{1,0:T(8,128)S(1)} %get-tuple-element.17.refs_2_, ...), custom_call_target="tpu_custom_call" | custom-call | tf_op jit(solution)/shard_map/pallas_call | solution.py:524

commit v5 on v4

--- a/solution.py
+++ b/solution.py
@@ -64,6 +64,7 @@
     t = lax.axis_index("tensor")
     mirror = sections - 1 - s
     after = sections - s
+    before = lax.rem(s - 1 + sections, sections)
     half = sections // 2
     toks, feats = down_rows.shape
     cols = down_grads.shape[1]
@@ -205,7 +206,7 @@
     def down_copy(c):
         part = pl.ds(c * step, step)
         return remote(
-            down_term.at[part], down_out.at[part], term_send.at[0, c], term_recv.at[0, c], (s - 1, t)
+            down_term.at[part], down_out.at[part], term_send.at[0, c], term_recv.at[0, c], (before, t)
         )
 
     def first_leg(c):

time: 91.6 us -> 91.6 us (level)
  no operation moved by 1% of the time
where the time goes in v5:
time: 91.6 us; the launch traced here: 91.5 us
  Pallas kernels  90.9 us (99%)
    pallas_call x1, Pallas kernels, relay(): pl.pallas_call(lambda *refs: relay_kernel(sections, ways, *refs), out_sha...  87.9 us
    pallas_call x1, Pallas kernels, leave(): pl.pallas_call(leave_kernel, out_shape=tuple((jax.ShapeDtypeStruct(x.shap...  3.01 us

profile of v5, /device:TPU:32, one launch (start us, length us, event | category | flops | bytes accessed | tf_op | source)
XLA Modules:
  0.0 91.5 jit_solution(9286082199352926505)
XLA Ops:
  0.6 87.9 %shard_map.110 = (f32[4096,128]{1,0:T(8,128)S(1)}, f32[4096,128]{1,0:T(8,128)S(1)}, f32[4096,128]{1,0:T(8,128)S(1)}, bf16[1024,256]{1,0:T(8,128)(2,1)S(1)}, bf16[1024,256]{1,0:T(8,128)(2,1)S(1)}) custom-call(bf16[4096,128]{1,0:T(8,128)(2,1)} %bitcast.14, f32[4096,128]{1,0:T(8,128)} %bitcast.12, f32[4096,128]{1,0:T(8,128)} %bitcast.13, ...), custom_call_target="tpu_custom_call" | custom-call | tf_op jit(solution)/shard_map/pallas_call | solution.py:475
  88.5 3.0 %shard_map.111 = (f32[4096,128]{1,0:T(8,128)}, f32[4096,128]{1,0:T(8,128)}, f32[4096,128]{1,0:T(8,128)}, bf16[1024,256]{1,0:T(8,128)(2,1)}, bf16[1024,256]{1,0:T(8,128)(2,1)}) custom-call(f32[4096,128]{1,0:T(8,128)S(1)} %get-tuple-element.15.refs_0_, f32[4096,128]{1,0:T(8,128)S(1)} %get-tuple-element.16.refs_1_, f32[4096,128]{1,0:T(8,128)S(1)} %get-tuple-element.17.refs_2_, ...), custom_call_target="tpu_custom_call" | custom-call | tf_op jit(solution)/shard_map/pallas_call | solution.py:525
